TPU v7x, 32 devices: a whole 2x2x4 slice. The times are simulated.
32 devices in a mesh: box: 2 (over x), theta: 4 (over y, core), phi: 4 (over z).
Axes of the slice: x: 2, y: 2, z: 4, core: 2. Of those that a mesh axis runs over, the one named last changes fastest.
Arguments:
- coeffs: bfloat16 [256, 2, 128, 256], P(('box', 'theta', 'phi')), may hold values from -6 to 6
- near_blocks: bfloat16 [256, 12, 2, 128, 128], P(('box', 'theta', 'phi')), may hold values from -0.109375 to 0.109375
- near_ids: int32 [256, 12], P(('box', 'theta', 'phi')), may hold values from 0 to 255, as said below
- near_count: int32 [256], P(('box', 'theta', 'phi')), may hold values from 3 to 12, as said below
- radiation: bfloat16 [256, 2, 128, 128], P(('box', 'theta', 'phi')), may hold values from -0.5 to 0.5
- partners: int32 [32, 16], P('box'), may hold values from 0 to 31, as said below
- vector_ids: int32 [32, 16], P('box'), may hold values from 0 to 315
- pair_count: int32 [32], P('box'), may hold values from 4 to 16, as said below
- translation: bfloat16 [316, 2, 16, 32], P(None, None, 'theta', 'phi'), may hold values from -0.5 to 0.5
Outputs:
- product: float32 [256, 2, 128, 256], P(('box', 'theta', 'phi'))
Inputs may be any that keep to these rules, and one draw needn't show every extreme that they name: `near_ids`: row b lists b itself first, then 12 - 1 further entries; the used ones (before near_count[b]) are distinct other leaf boxes whose index differs from b by at most 8, and some used entry differs by exactly 8. Entries at or after near_count[b] are not used and may repeat b. `near_count`: some leaf box uses all 12 slots. `partners`: row d holds 16 distinct upper boxes other than d whose index differs from d by at most 16; a difference of exactly 16 occurs among used entries. Entries at or after pair_count[d] are not used. `pair_count`: some upper box uses all 16 slots.
All inputs are finite; a program needn't handle non-finite values.
Results may differ from a plain program's by a relative error of at most 0.0055.
Values may be sent and summed in bfloat16 or wider, within the bound.
No kernel may reach another device: no remote copies, remote signals or barrier semaphores. Data moves between devices by JAX's collectives and lax.ppermute only.
A program may use at most 128 MiB of HBM per device.

v0:
```python
import functools
import math

import jax
import jax.numpy as jnp
import ml_dtypes
import numpy as np
from jax import lax
from jax.experimental import pallas as pl
from jax.experimental.pallas import tpu as pltpu
from jax.sharding import PartitionSpec as P

TL = 8
PL = 16
TU = 16
PU = 32

WEIGHT_UP = (-0.0546875, 0.8203125, 0.2734375, -0.0390625)
WEIGHT_DOWN = (-0.0390625, 0.2734375, 0.8203125, -0.0546875)
PHASE_SCALE = 1.3

F32 = jnp.float32
BF16 = jnp.bfloat16
MIB = 2**20
GROUP = 2
NOWHERE = -(2**20)


def lagrange(rows, columns, wrap):
    matrix = np.zeros((rows, columns))
    for row in range(rows):
        weights = WEIGHT_UP if row % 2 else WEIGHT_DOWN
        for order in range(4):
            node = row // 2 + row % 2 - 2 + order
            node = node % columns if wrap else min(max(node, 0), columns - 1)
            matrix[row, node] += weights[order]
    return matrix


def split_weights(matrix):
    high = matrix.astype(ml_dtypes.bfloat16)
    low = (matrix - high.astype(np.float64)).astype(ml_dtypes.bfloat16)
    return high, low


def operators(shares, theta_size, phi_size):
    theta_part = TU // theta_size // shares
    order = np.arange(TU * PU).reshape(theta_size, shares, theta_part, phi_size, PU // phi_size)
    order = order.transpose(1, 0, 3, 2, 4).reshape(-1)
    interp = np.kron(lagrange(TU, TL, False), lagrange(PU, PL, True))
    theta = math.pi * (np.arange(TU) + 0.5) / TU
    azimuth = 2.0 * math.pi * (np.arange(PU) + 0.5) / PU
    up, down = [], []
    for octant in range(4):
        sign_x = 2 * (octant % 2) - 1
        sign_y = 2 * (octant // 2 % 2) - 1
        sign_z = 2 * (octant // 4) - 1
        angle = PHASE_SCALE * (
            sign_x * np.sin(theta)[:, None] * np.cos(azimuth)[None]
            + sign_y * np.sin(theta)[:, None] * np.sin(azimuth)[None]
            + sign_z * np.cos(theta)[:, None]
        ).reshape(-1, 1)
        cos_high, cos_low = split_weights((np.cos(angle) * interp)[order])
        sin_high, sin_low = split_weights((np.sin(angle) * interp)[order])
        high = np.concatenate([cos_high, sin_high], axis=1)
        low = np.concatenate([cos_low, sin_low], axis=1)
        up.append(np.concatenate([high, low], axis=0))
        down += [cos_high.T, sin_high.T]
    return np.concatenate(up, axis=1), np.concatenate(down, axis=0)


def in_hbm(*arrays):
    return [pltpu.with_memory_space_constraint(array, pltpu.HBM) for array in arrays]


def dot(a, b):
    return jnp.dot(a, b, preferred_element_type=F32)


def side_by_side(real, imag):
    return jnp.concatenate([real, imag], axis=1)


def complex_columns(real, imag):
    return jnp.concatenate([side_by_side(real, imag), side_by_side(-imag, real)], axis=0)


def up_kernel(x_hbm, rad_hbm, w_hbm, out_hbm, x_ref, rad_ref, w_ref, right, result, sems):
    boxes, _, _, rhs = x_ref.shape
    points = rad_ref.shape[2]
    copies = [
        pltpu.make_async_copy(source, target, sems.at[place])
        for place, (source, target) in enumerate(
            ((x_hbm, x_ref), (rad_hbm, rad_ref), (w_hbm, w_ref))
        )
    ]
    for copy in copies:
        copy.start()
    copies[0].wait()
    copies[1].wait()
    half = boxes // 2
    for octant in range(boxes):
        left = side_by_side(rad_ref[octant, 0], rad_ref[octant, 1])
        straight = dot(left, complex_columns(x_ref[octant, 0], x_ref[octant, 1])).astype(BF16)
        real, imag = straight[:, :rhs], straight[:, rhs:]
        if octant < half:
            swapped = side_by_side(-imag, real)
        else:
            swapped = side_by_side(imag, -real)
        place = octant if octant < half else boxes - 1 - octant
        start = 2 * place * points
        right[octant // half, start : start + points] = straight
        right[octant // half, start + points : start + 2 * points] = swapped
    copies[2].wait()
    total = dot(w_ref[...], right[0]) + dot(w_ref[...], right[1])
    samples = total.shape[0] // 2
    total = total[:samples] + total[samples:]
    result[...] = total.astype(BF16).reshape(result.shape)
    pltpu.sync_copy(result, out_hbm)


def upward(coeffs, radiation, weights, groups):
    boxes, _, basis, rhs = coeffs.shape
    rows, columns = weights.shape
    samples = rows // 2
    hbm = pl.BlockSpec(memory_space=pltpu.HBM)
    return pl.pallas_call(
        up_kernel,
        in_specs=[hbm] * 3,
        out_specs=hbm,
        out_shape=pltpu.HBM((groups, samples // groups, 2 * rhs), BF16),
        scratch_shapes=[
            pltpu.VMEM(coeffs.shape, BF16),
            pltpu.VMEM(radiation.shape, BF16),
            pltpu.VMEM(weights.shape, BF16),
            pltpu.VMEM((2, columns, 2 * rhs), BF16),
            pltpu.VMEM((groups, samples // groups, 2 * rhs), BF16),
            pltpu.SemaphoreType.DMA((3,)),
        ],
        compiler_params=pltpu.CompilerParams(vmem_limit_bytes=32 * MIB),
        cost_estimate=pl.CostEstimate(
            flops=10**6, bytes_accessed=2**10, transcendentals=0
        ),
        name="upward",
    )(*in_hbm(coeffs, radiation, weights))


def coupling_kernel(lists_ref, base_ref, table_ref, out_ref):
    rows = lists_ref.shape[0]
    samples = table_ref.shape[1] // 2
    _, targets, columns = out_ref.shape
    slots = rows // targets
    selector = (
        lax.broadcasted_iota(jnp.int32, (rows, table_ref.shape[0]), 1) == lists_ref[:, 1:2]
    )
    chosen = dot(selector.astype(BF16), table_ref[...]).astype(BF16)
    wide = lax.broadcasted_iota(jnp.int32, (rows, columns), 1) // samples
    match = wide + base_ref[0] == lists_ref[:, 0:1]
    spread = lax.broadcasted_iota(jnp.int32, (samples, columns), 0) == (
        lax.broadcasted_iota(jnp.int32, (samples, columns), 1) % samples
    )
    gather = (
        lax.broadcasted_iota(jnp.int32, (targets, rows), 1) // slots
        == lax.broadcasted_iota(jnp.int32, (targets, rows), 0)
    ).astype(BF16)
    tile = spread.astype(BF16)
    for part in range(2):
        lines = dot(chosen[:, part * samples : (part + 1) * samples], tile)
        out_ref[part] = dot(gather, jnp.where(match, lines, 0.0).astype(BF16))


def couplings(lists, base, table, targets, names):
    shape = (2, targets, names * (table.shape[1] // 2))
    vmem = pl.BlockSpec(memory_space=pltpu.VMEM)
    return pl.pallas_call(
        coupling_kernel,
        in_specs=[vmem, pl.BlockSpec(memory_space=pltpu.SMEM), vmem],
        out_specs=vmem,
        out_shape=jax.ShapeDtypeStruct(shape, F32),
        compiler_params=pltpu.CompilerParams(vmem_limit_bytes=16 * MIB),
        cost_estimate=pl.CostEstimate(
            flops=2 * 10**8, bytes_accessed=2 * 2**20, transcendentals=0
        ),
        name="coupling",
    )(lists, base, table)


def translate_kernel(lines_hbm, *refs):
    count = (len(refs) - 5) // 2
    sources, out_hbm = refs[:count], refs[count]
    held, lines, matrix, result, sems = refs[count + 1 :][:count], *refs[2 * count + 1 :]
    targets, samples, width = result.shape
    rhs = width // 2
    copies = [
        pltpu.make_async_copy(source, target, sems.at[place])
        for place, (source, target) in enumerate(zip((lines_hbm, *sources), (lines, *held)))
    ]
    for copy in copies:
        copy.start()
    copies[0].wait()
    columns = matrix.shape[1]
    row = lax.broadcasted_iota(jnp.int32, (samples, columns), 0)
    diagonal = row == lax.broadcasted_iota(jnp.int32, (samples, columns), 1) % samples
    for part in range(2):
        for target in range(targets):
            line = jnp.broadcast_to(lines[part, target : target + 1], diagonal.shape)
            start = (part * targets + target) * samples
            matrix[start : start + samples] = jnp.where(diagonal, line, 0.0).astype(BF16)
    total = None
    start = 0
    for place, source in enumerate(held):
        copies[1 + place].wait()
        stop = start + source.shape[0] * samples
        part = dot(matrix[:, start:stop], source[...].reshape(stop - start, width))
        total = part if total is None else total + part
        start = stop
    half = targets * samples
    real = total[:half, :rhs] - total[half:, rhs:]
    imag = total[:half, rhs:] + total[half:, :rhs]
    result[...] = jnp.concatenate([real, imag], axis=1).astype(BF16).reshape(result.shape)
    pltpu.sync_copy(result, out_hbm)


def translate(lines, sources):
    _, samples, width = sources[0].shape
    _, targets, columns = lines.shape
    shape = (targets, samples, width)
    hbm = pl.BlockSpec(memory_space=pltpu.HBM)
    anywhere = pl.BlockSpec(memory_space=pl.ANY)
    return pl.pallas_call(
        translate_kernel,
        in_specs=[hbm] + [anywhere] * len(sources),
        out_specs=hbm,
        out_shape=pltpu.HBM(shape, BF16),
        scratch_shapes=[
            *[pltpu.VMEM(source.shape, BF16) for source in sources],
            pltpu.VMEM(lines.shape, F32),
            pltpu.VMEM((2 * targets * samples, columns), BF16),
            pltpu.VMEM(shape, BF16),
            pltpu.SemaphoreType.DMA((1 + len(sources),)),
        ],
        compiler_params=pltpu.CompilerParams(vmem_limit_bytes=24 * MIB),
        cost_estimate=pl.CostEstimate(
            flops=10**6, bytes_accessed=2**10, transcendentals=0
        ),
        name="translate",
    )(*in_hbm(lines), *sources)


def near_kernel(first, begun, kept, *refs):
    count = 1 if first == 1 else 2
    listed, starts_ref, blocks_hbm = refs[:3]
    source_refs, refs = refs[3 : 3 + count], refs[3 + count :]
    before_hbm = refs[0] if begun else None
    kept_hbm = refs[begun : begun + kept]
    out_ref = refs[begun + kept]
    kept_refs = refs[1 + begun + kept : 1 + begun + 2 * kept]
    blocks, held, wide, total_ref, sems = refs[1 + begun + 2 * kept :]
    boxes, _, basis, rhs = held.shape
    most = blocks_hbm.shape[0]
    starts = [starts_ref[first, box] for box in range(boxes + 1)]

    def by_box(source, target, turn):
        return [
            pltpu.make_async_copy(
                source.at[box], target.at[box], sems.at[most + turn * boxes + box]
            )
            for box in range(boxes)
        ]

    part = boxes // count
    source_copies = [
        pltpu.make_async_copy(
            source_refs[box // part].at[box % part], held.at[box], sems.at[most + box]
        )
        for box in range(boxes)
    ]
    before_copies = by_box(before_hbm, total_ref, 1) if begun else []
    out_copies = [] if kept else by_box(total_ref, out_ref, 2)
    kept_copies = [
        pltpu.make_async_copy(kept_hbm[place], kept_refs[place], sems.at[most + 3 * boxes + place])
        for place in range(kept)
    ]
    for copy in source_copies:
        copy.start()

    def block_copy(place):
        block = listed[first, place] // boxes
        return pltpu.make_async_copy(blocks_hbm.at[block], blocks.at[place], sems.at[place])

    def fetch(place, carry):
        block_copy(place).start()
        return carry

    lax.fori_loop(0, starts[boxes], fetch, 0)
    for copy in before_copies + kept_copies:
        copy.start()
    for copy in source_copies:
        copy.wait()
    for place in range(boxes):
        wide[place] = complex_columns(held[place, 0], held[place, 1])

    def landed(place, carry):
        block_copy(place).wait()
        return carry

    lax.fori_loop(0, starts[boxes], landed, 0)
    for copy in before_copies:
        copy.wait()

    def group(box, begin, size):
        left, right = [], []
        for step in range(size):
            place = starts[box] + begin + step
            valid = place < starts[box + 1]
            place = jnp.where(valid, place, 0)
            real, imag = blocks[place, 0], blocks[place, 1]
            real = jnp.where(valid, real, jnp.zeros_like(real))
            imag = jnp.where(valid, imag, jnp.zeros_like(imag))
            left.append(side_by_side(real, imag))
            right.append(wide[jnp.where(valid, listed[first, place] % boxes, 0)])
        return dot(jnp.concatenate(left, axis=1), jnp.concatenate(right, axis=0))

    half = boxes // 2
    possible = [
        (
            min(half, boxes - box) + min(half, box + 1),
            boxes,
            max(half - box, 0) + max(box + 1 - half, 0),
        )[first]
        for box in range(boxes)
    ]
    sizes = [min(most_sources, 3 if most_sources < 7 else 4) for most_sources in possible]
    for box in range(boxes):
        part = group(box, 0, sizes[box])
        if begun:
            total_ref[box, 0] += part[:, :rhs]
            total_ref[box, 1] += part[:, rhs:]
        else:
            total_ref[box, 0] = part[:, :rhs]
            total_ref[box, 1] = part[:, rhs:]
    for box in range(boxes):

        def more(index, carry, box=box):
            part = group(box, sizes[box] + GROUP * index, GROUP)
            total_ref[box, 0] += part[:, :rhs]
            total_ref[box, 1] += part[:, rhs:]
            return carry

        rest = starts[box + 1] - starts[box] - sizes[box]
        lax.fori_loop(0, (jnp.maximum(rest, 0) + GROUP - 1) // GROUP, more, 0)
        if out_copies:
            out_copies[box].start()
    for copy in out_copies + kept_copies:
        copy.wait()


def near_slots(ids, used, rank):
    boxes, slots = ids.shape
    total = boxes * slots
    source = ids - (rank - 1) * boxes
    source = jnp.where(jnp.arange(slots) < used[:, None], source, -1).reshape(-1)
    half = boxes // 2
    side, inside = source // boxes, source % boxes
    near = ((side == 0) & (inside >= half)) | ((side == 2) & (inside < half))
    far = ((side == 0) & (inside < half)) | ((side == 2) & (inside >= half))
    wanted = (source >= 0) & jnp.stack([near, side == 1, far])
    inside = jnp.where(near, (inside + half) % boxes, inside)
    earlier = jnp.arange(total)[None, :] < jnp.arange(total)[:, None]
    place = jnp.sum((wanted[:, None, :] & earlier).astype(jnp.int32), axis=2)
    code = jnp.arange(total) * boxes + inside
    chosen = wanted[:, None, :] & (place[:, None, :] == jnp.arange(total)[:, None])
    listed = jnp.sum(jnp.where(chosen, code, 0), axis=2)
    before = jnp.arange(total) // slots < jnp.arange(boxes + 1)[:, None]
    starts = jnp.sum((wanted[:, None, :] & before).astype(jnp.int32), axis=2)
    return listed.astype(jnp.int32), starts.astype(jnp.int32)


def near_field(listed, starts, blocks, sources, first, before=None, keep=()):
    boxes, slots, _, basis, _ = blocks.shape
    blocks = blocks.reshape(boxes * slots, *blocks.shape[2:])
    rhs = sources[0].shape[3]
    begun, kept = before is not None, len(keep)
    hbm = pl.BlockSpec(memory_space=pltpu.HBM)
    smem = pl.BlockSpec(memory_space=pltpu.SMEM)
    vmem = pl.BlockSpec(memory_space=pltpu.VMEM)
    shape = (boxes, 2, basis, rhs)
    scratch = [
        pltpu.VMEM(blocks.shape, BF16),
        pltpu.VMEM(shape, BF16),
        pltpu.VMEM((boxes, 2 * basis, 2 * rhs), BF16),
        pltpu.VMEM(shape, F32),
        pltpu.SemaphoreType.DMA((boxes * slots + 3 * boxes + kept,)),
    ]
    kernel = functools.partial(near_kernel, first, begun, kept)
    if kept:
        del scratch[3]
        inner = kernel

        def kernel(*refs):
            place = 3 + len(sources) + begun + kept
            inner(*refs[:-1], refs[place], refs[-1])

    return pl.pallas_call(
        kernel,
        in_specs=[smem] * 2
        + [hbm]
        + [pl.BlockSpec(memory_space=pl.ANY)] * len(sources)
        + [hbm] * (begun + kept),
        out_specs=[vmem] * (1 + kept) if kept else hbm,
        out_shape=[
            pltpu.VMEM(shape, F32),
            *[pltpu.VMEM(array.shape, array.dtype) for array in keep],
        ]
        if kept
        else pltpu.HBM(shape, F32),
        scratch_shapes=scratch,
        compiler_params=pltpu.CompilerParams(vmem_limit_bytes=32 * MIB),
        cost_estimate=pl.CostEstimate(
            flops=10**6 if first == 1 else 10**11, bytes_accessed=2**10, transcendentals=0
        ),
        name=("near_nearer", "near_own", "near_farther")[first],
    )(
        listed,
        starts,
        *in_hbm(blocks),
        *(sources if first != 1 else in_hbm(*sources)),
        *in_hbm(*([before] if begun else []), *keep),
    )


def adjoint_kernel(rad_ref, out_hbm, held):
    for box in range(rad_ref.shape[0]):
        held[box] = side_by_side(rad_ref[box, 0].T, rad_ref[box, 1].T)
    pltpu.sync_copy(held, out_hbm)


def adjoint(radiation):
    boxes, _, points, basis = radiation.shape
    return pl.pallas_call(
        adjoint_kernel,
        in_specs=[pl.BlockSpec(memory_space=pltpu.VMEM)],
        out_specs=pl.BlockSpec(memory_space=pltpu.HBM),
        scratch_shapes=[pltpu.VMEM((boxes, basis, 2 * points), BF16)],
        out_shape=pltpu.HBM((boxes, basis, 2 * points), BF16),
        cost_estimate=pl.CostEstimate(
            flops=10**6, bytes_accessed=2**10, transcendentals=0
        ),
        name="adjoint",
    )(radiation)


def down_kernel(near_ref, w_ref, adjoint_ref, field_ref, out_hbm, field, held, sems):
    boxes, _, width = adjoint_ref.shape
    points = width // 2
    rhs = held.shape[3]
    field_copy = pltpu.make_async_copy(field_ref, field, sems.at[boxes])
    field_copy.start()
    out_copies = [
        pltpu.make_async_copy(held.at[box], out_hbm.at[box], sems.at[box]) for box in range(boxes)
    ]
    field_copy.wait()
    mixed = dot(w_ref[...], field[...].reshape(w_ref.shape[1], 2 * rhs))
    for octant in range(boxes // 2):
        start = 2 * octant * points
        cos_part = mixed[start : start + points]
        sin_part = mixed[start + points : start + 2 * points]
        cos_re, cos_im = cos_part[:, :rhs], cos_part[:, rhs:]
        sin_re, sin_im = sin_part[:, :rhs], sin_part[:, rhs:]
        leaves = (
            (octant, cos_re + sin_im, cos_im - sin_re),
            (boxes - 1 - octant, cos_re - sin_im, cos_im + sin_re),
        )
        for box, real, imag in leaves:
            real, imag = real.astype(BF16), imag.astype(BF16)
            right = jnp.concatenate([side_by_side(real, imag), side_by_side(imag, -real)], axis=0)
            far = dot(adjoint_ref[box], right)
            held[box, 0] = near_ref[box, 0] + far[:, :rhs]
            held[box, 1] = near_ref[box, 1] + far[:, rhs:]
            out_copies[box].start()
    for copy in out_copies:
        copy.wait()


def downward(field, near, weights, radiation_adjoint):
    boxes = near.shape[0]
    ready = [
        pltpu.with_memory_space_constraint(array, pltpu.VMEM)
        for array in (near, weights, radiation_adjoint)
    ]
    return pl.pallas_call(
        down_kernel,
        in_specs=[pl.BlockSpec(memory_space=pltpu.VMEM)] * 3
        + [pl.BlockSpec(memory_space=pl.ANY)],
        out_specs=pl.BlockSpec(memory_space=pltpu.HBM),
        out_shape=jax.ShapeDtypeStruct(near.shape, F32),
        scratch_shapes=[
            pltpu.VMEM(field.shape, BF16),
            pltpu.VMEM(near.shape, F32),
            pltpu.SemaphoreType.DMA((boxes + 1,)),
        ],
        compiler_params=pltpu.CompilerParams(vmem_limit_bytes=32 * MIB),
        cost_estimate=pl.CostEstimate(
            flops=10**6, bytes_accessed=2**10, transcendentals=0
        ),
        name="downward",
    )(*ready, field)


def shift(block, axis, step):
    count = lax.axis_size(axis)
    pairs = [(i, i + step) for i in range(count) if 0 <= i + step < count]
    return lax.ppermute(block, axis, pairs)


def lists_of(partners, vector_ids, pair_count):
    used = jnp.arange(partners.shape[1])[None, :] < pair_count[:, None]
    names = jnp.where(used, partners, NOWHERE)
    return jnp.stack([names, vector_ids], axis=2).reshape(-1, 2)


def parent_bands(spread, shares):
    axes = ("box", "theta", "phi") if shares == lax.axis_size("box") else ("theta", "phi")
    return lax.all_to_all(spread, axes, split_axis=0, concat_axis=0, tiled=True)


def translation_lines(lists, translation, shares, per_group):
    operator_total, _, theta_band, phi_band = translation.shape
    rank = lax.axis_index("box")
    if shares < lax.axis_size("box"):
        table = translation.reshape(operator_total, -1)
        base = ((rank - 1) * per_group).astype(jnp.int32).reshape(1)
        return couplings(lists, base, table, per_group, 3 * per_group)
    if shares == 2:
        other = lax.ppermute(lists, "box", [(0, 1), (1, 0)])
        lists = jnp.where(
            rank == 0, jnp.concatenate([lists, other]), jnp.concatenate([other, lists])
        )
    part = theta_band // shares
    table = lax.dynamic_slice_in_dim(translation, rank * part, part, axis=2)
    table = table.reshape(operator_total, -1)
    total = shares * per_group
    return couplings(lists, jnp.zeros((1,), jnp.int32), table, total, total)


def per_device(
    shares,
    up_weights,
    down_weights,
    coeffs,
    near_blocks,
    near_ids,
    near_count,
    radiation,
    partners,
    vector_ids,
    pair_count,
    translation,
):
    every = ("box", "theta", "phi")
    per_group = lax.axis_size("theta") * lax.axis_size("phi")
    half = coeffs.shape[0] // 2
    front, back = coeffs[:half], coeffs[half:]
    nearer = (shift(back, every, 1), shift(front, every, -1))
    spread = upward(coeffs, radiation, up_weights, shares * per_group)
    radiation_adjoint = adjoint(radiation)
    lists = lists_of(partners, vector_ids, pair_count)
    spread, lists = lax.optimization_barrier((spread, lists))
    lines = translation_lines(lists, translation, shares, per_group)
    listed, starts = near_slots(near_ids, near_count, lax.axis_index(every))
    spread, lines, radiation_adjoint, listed, starts = lax.optimization_barrier(
        (spread, lines, radiation_adjoint, listed, starts)
    )
    parents = parent_bands(spread, shares)
    near = near_field(listed, starts, near_blocks, nearer, 0)
    near, front, back = lax.optimization_barrier((near, front, back))
    farther = (shift(front, every, 1), shift(back, every, -1))
    parents, near = lax.optimization_barrier((parents, near))
    sources = [parents]
    if shares < lax.axis_size("box"):
        sources = [shift(parents, "box", 1), parents, shift(parents, "box", -1)]
    incoming = translate(lines, sources)
    incoming, near = lax.optimization_barrier((incoming, near))
    field = parent_bands(incoming, shares)
    near = near_field(listed, starts, near_blocks, (coeffs,), 1, near)
    ready = near_field(
        listed, starts, near_blocks, farther, 2, near, keep=(down_weights, radiation_adjoint)
    )
    return downward(field, *ready)


def solution(mesh):
    box_size, theta_size, phi_size = (mesh.shape[axis] for axis in ("box", "theta", "phi"))
    shares = box_size if box_size <= 2 and TU // theta_size % box_size == 0 else 1
    up_weights, down_weights = operators(shares, theta_size, phi_size)
    in_specs = (
        P(),
        P(),
        P(("box", "theta", "phi"), None, None, None),
        P(("box", "theta", "phi"), None, None, None, None),
        P(("box", "theta", "phi"), None),
        P(("box", "theta", "phi")),
        P(("box", "theta", "phi"), None, None, None),
        P("box", None),
        P("box", None),
        P("box"),
        P(None, None, "theta", "phi"),
    )
    out_specs = P(("box", "theta", "phi"), None, None, None)
    mapped = jax.shard_map(
        functools.partial(per_device, shares),
        mesh=mesh,
        in_specs=in_specs,
        out_specs=out_specs,
        check_vma=False,
    )

    def product(*arrays):
        return mapped(jnp.asarray(up_weights), jnp.asarray(down_weights), *arrays)

    return product
```

profile of v0, /device:TPU:0, one launch (start us, length us, event | category | flops | bytes accessed | tf_op | source)
XLA Modules:
  0.0 90.6 jit_solution(10049167050395686653)
XLA Ops:
  0.0 0.8 stack.16
  0.8 0.8 fusion.1
  1.7 5.3 %upward.1 = bf16[32,16,512]{2,1,0:T(8,128)(2,1)} custom-call(bf16[8,2,128,256]{3,2,1,0:T(8,128)(2,1)} %refs_3_.1, bf16[8,2,128,128]{3,2,1,0:T(8,128)(2,1)} %rad_ref.1, bf16[1024,1024]{1,0:T(8,128)(2,1)} %constant.77.clone.w_hbm), custom_call_target="tpu_custom_call" | custom-call | flops 1000000 | bytes 1024 | tf_op jit(solution)/shard_map/upward/pallas_call | solution.py:127
  7.0 3.0 %collective-permute-start = (s32[256,2]{0,1:T(2,128)S(1)}, s32[256,2]{0,1:T(2,128)S(1)}, u32[]{:S(2)}, u32[]{:S(2)}) collective-permute-start(s32[256,2]{0,1:T(2,128)S(1)} %pad_add_fusion.2), channel_id=1, source_target_pairs={{0,16},{16,0},{1,17},{17,1},{2,18},{18,2},{3,19},{19,3},{4,20},{20... | collective-permute-start | bytes 6152 | tf_op jit(solution)/shard_map/ppermute | solution.py:535
  10.1 1.3 %collective-permute-start.2 = (bf16[4,2,128,256]{3,2,1,0:T(8,128)(2,1)S(1)}, bf16[4,2,128,256]{3,2,1,0:T(8,128)(2,1)S(1)}, u32[]{:S(2)}, u32[]{:S(2)}) collective-permute-start(bf16[4,2,128,256]{3,2,1,0:T(8,128)(2,1)S(1)} %get-tuple-element.26), channel_id=1, source_target_pairs={{1,0},{2,1},{3,2},{4,3},{5,4},{6,5},{7,6},{8,7},{9,8},{10,9},{11,1... | collective-permute-start | bytes 1572872 | tf_op jit(solution)/shard_map/ppermute | solution.py:513
  11.4 4.6 %collective-permute-start.1 = (bf16[4,2,128,256]{3,2,1,0:T(8,128)(2,1)S(1)}, bf16[4,2,128,256]{3,2,1,0:T(8,128)(2,1)S(1)}, u32[]{:S(2)}, u32[]{:S(2)}) collective-permute-start(bf16[4,2,128,256]{3,2,1,0:T(8,128)(2,1)S(1)} %get-tuple-element.27), channel_id=1, source_target_pairs={{0,1},{1,2},{2,3},{3,4},{4,5},{5,6},{6,7},{7,8},{8,9},{9,10},{10,1... | collective-permute-start | bytes 1572872 | tf_op jit(solution)/shard_map/ppermute | solution.py:513
  16.4 0.1 convert_reduce_fusion
  16.5 0.2 select_reduce_fusion.refs_0_
  16.7 0.2 convert_reduce_fusion.1
  17.1 2.0 %adjoint.1.refs_7_ = bf16[8,128,256]{2,1,0:T(8,128)(2,1)} custom-call(bf16[8,2,128,128]{3,2,1,0:T(8,128)(2,1)} %rad_ref.1), custom_call_target="tpu_custom_call" | custom-call | flops 1000000 | bytes 1024 | tf_op jit(solution)/shard_map/adjoint/pallas_call | solution.py:440
  19.1 0.1 copy.20
  19.3 0.1 copy.19
  19.5 1.1 %coupling.1.lines_hbm = f32[2,32,512]{2,1,0:T(8,128)S(1)} custom-call(s32[512,2]{1,0:T(8,128)S(1)} %broadcast_select_fusion.lists_ref, s32[1]{0:T(128)} %constant.65.clone.1.base_ref, bf16[316,32]{1,0:T(8,128)(2,1)S(1)} %copy.21.table_ref), custom_call_target="tpu_custom_call" | custom-call | flops 200000000 | bytes 2097152 | tf_op jit(solution)/shard_map/coupling/pallas_call | solution.py:175
  20.6 0.7 copy-done.3
  21.3 7.4 %all-to-all-start = ((bf16[32,16,512]{2,1,0:T(8,128)(2,1)}), bf16[32,16,512]{2,1,0:T(8,128)(2,1)S(1)}, u32[]{:S(2)}, u32[]{:S(2)}) async-start(bf16[32,16,512]{2,1,0:T(8,128)(2,1)} %upward.1), calls=%async_computation | async-start | bytes 1048576 | tf_op jit(solution)/shard_map/all_to_all | solution.py:524
  28.7 6.7 %near_nearer.1.refs_4_ = f32[8,2,128,256]{3,2,1,0:T(8,128)} custom-call(s32[3,96]{1,0:T(4,128)S(1)} %select_reduce_fusion.refs_0_, s32[3,9]{1,0:T(4,128)S(1)} %copy.24.refs_1_, bf16[96,2,128,128]{3,2,1,0:T(8,128)(2,1)} %bitcast.2, bf16[4,2,128,256]{3,2,1,0:T(8,128)(2,1)S(1)} %collective-permute-done.1.refs_3_, ...), custom_call_target="tpu_custom_call" | custom-call | flops 99999997952 | bytes 1024 | tf_op jit(solution)/shard_map/near_nearer/pallas_call | solution.py:404
  35.4 9.3 %collective-permute-start.3 = (bf16[4,2,128,256]{3,2,1,0:T(8,128)(2,1)S(1)}, bf16[4,2,128,256]{3,2,1,0:T(8,128)(2,1)S(1)}, u32[]{:S(2)}, u32[]{:S(2)}) collective-permute-start(bf16[4,2,128,256]{3,2,1,0:T(8,128)(2,1)S(1)} %get-tuple-element.26), channel_id=1, source_target_pairs={{0,1},{1,2},{2,3},{3,4},{4,5},{5,6},{6,7},{7,8},{8,9},{9,10},{10,1... | collective-permute-start | bytes 1572872 | tf_op jit(solution)/shard_map/ppermute | solution.py:513
  44.7 1.3 %collective-permute-start.4 = (bf16[4,2,128,256]{3,2,1,0:T(8,128)(2,1)S(1)}, bf16[4,2,128,256]{3,2,1,0:T(8,128)(2,1)S(1)}, u32[]{:S(2)}, u32[]{:S(2)}) collective-permute-start(bf16[4,2,128,256]{3,2,1,0:T(8,128)(2,1)S(1)} %get-tuple-element.27), channel_id=1, source_target_pairs={{1,0},{2,1},{3,2},{4,3},{5,4},{6,5},{7,6},{8,7},{9,8},{10,9},{11,1... | collective-permute-start | bytes 1572872 | tf_op jit(solution)/shard_map/ppermute | solution.py:513
  46.0 3.7 %all-to-all-done.refs_0_ = bf16[32,16,512]{2,1,0:T(8,128)(2,1)S(1)} async-done(((bf16[32,16,512]{2,1,0:T(8,128)(2,1)}), bf16[32,16,512]{2,1,0:T(8,128)(2,1)S(1)}, u32[]{:S(2)}, u32[]{:S(2)}) %all-to-all-start) | async-done | bytes 524320 | tf_op jit(solution)/shard_map/all_to_all | solution.py:524
  49.7 2.5 %translate.1 = bf16[32,16,512]{2,1,0:T(8,128)(2,1)} custom-call(f32[2,32,512]{2,1,0:T(8,128)} %copy-done.3, bf16[32,16,512]{2,1,0:T(8,128)(2,1)S(1)} %all-to-all-done.refs_0_), custom_call_target="tpu_custom_call" | custom-call | flops 1000000 | bytes 1024 | tf_op jit(solution)/shard_map/translate/pallas_call | solution.py:230
  52.2 7.7 %all-to-all-start.1 = ((bf16[32,16,512]{2,1,0:T(8,128)(2,1)}), bf16[32,16,512]{2,1,0:T(8,128)(2,1)S(1)}, u32[]{:S(2)}, u32[]{:S(2)}) async-start(bf16[32,16,512]{2,1,0:T(8,128)(2,1)} %translate.1), calls=%async_computation.1 | async-start | bytes 1048576 | tf_op jit(solution)/shard_map/all_to_all | solution.py:524
  59.9 8.6 %near_own.1.refs_5_ = f32[8,2,128,256]{3,2,1,0:T(8,128)} custom-call(s32[3,96]{1,0:T(4,128)S(1)} %select_reduce_fusion.refs_0_, s32[3,9]{1,0:T(4,128)S(1)} %copy.24.refs_1_, bf16[96,2,128,128]{3,2,1,0:T(8,128)(2,1)} %bitcast.3, bf16[8,2,128,256]{3,2,1,0:T(8,128)(2,1)} %refs_3_.1, f32[8,2,128,256]{3,2,1,0:T(8,128)} %near_nearer.1.refs_4_), custom_call_target="tpu_custom_call" | custom-call | flops 1000000 | bytes 1024 | tf_op jit(solution)/shard_map/near_own/pallas_call | solution.py:404
  68.6 0.8 copy-done.4
  69.3 2.0 %collective-permute-done.4.refs_4_ = bf16[4,2,128,256]{3,2,1,0:T(8,128)(2,1)S(1)} collective-permute-done((bf16[4,2,128,256]{3,2,1,0:T(8,128)(2,1)S(1)}, bf16[4,2,128,256]{3,2,1,0:T(8,128)(2,1)S(1)}, u32[]{:S(2)}, u32[]{:S(2)}) %collective-permute-start.4) | collective-permute-done | bytes 524320 | tf_op jit(solution)/shard_map/ppermute | solution.py:513
  71.3 0.8 copy-done.6
  72.1 1.0 %copy-done.5 = bf16[4,2,128,256]{3,2,1,0:T(8,128)(2,1)S(1)} copy-done((bf16[4,2,128,256]{3,2,1,0:T(8,128)(2,1)S(1)}, bf16[4,2,128,256]{3,2,1,0:T(8,128)(2,1)}, u32[]{:S(2)}) %copy-start.5) | copy-done | bytes 524312
  73.2 1.0 %copy-done.7 = bf16[4,2,128,256]{3,2,1,0:T(8,128)(2,1)S(1)} copy-done((bf16[4,2,128,256]{3,2,1,0:T(8,128)(2,1)S(1)}, bf16[4,2,128,256]{3,2,1,0:T(8,128)(2,1)}, u32[]{:S(2)}) %copy-start.7) | copy-done | bytes 524312
  74.2 5.7 %near_farther.1 = (f32[8,2,128,256]{3,2,1,0:T(8,128)S(1)}, bf16[1024,512]{1,0:T(8,128)(2,1)S(1)}, bf16[8,128,256]{2,1,0:T(8,128)(2,1)S(1)}) custom-call(s32[3,96]{1,0:T(4,128)S(1)} %select_reduce_fusion.refs_0_, s32[3,9]{1,0:T(4,128)S(1)} %copy.24.refs_1_, bf16[96,2,128,128]{3,2,1,0:T(8,128)(2,1)} %bitcast.4, bf16[4,2,128,256]{3,2,1,0:T(8,128)(2,1)S(1)} %copy-done.5, ...), custom_call_target="tpu_custom_call" | custom-call | flops 99999997952 | bytes 1024 | tf_op jit(solution)/shard_map/near_farther/pallas_call | solution.py:404
  79.9 1.0 %copy-done.1 = bf16[1024,512]{1,0:T(8,128)(2,1)} copy-done((bf16[1024,512]{1,0:T(8,128)(2,1)}, bf16[1024,512]{1,0:T(8,128)(2,1)S(1)}, u32[]{:S(2)}) %copy-start.1) | copy-done | bytes 1048600
  80.9 6.3 %all-to-all-done.1.field_ref = bf16[32,16,512]{2,1,0:T(8,128)(2,1)S(1)} async-done(((bf16[32,16,512]{2,1,0:T(8,128)(2,1)}), bf16[32,16,512]{2,1,0:T(8,128)(2,1)S(1)}, u32[]{:S(2)}, u32[]{:S(2)}) %all-to-all-start.1) | async-done | bytes 524320 | tf_op jit(solution)/shard_map/all_to_all | solution.py:524
  87.2 1.2 %copy-done.2 = bf16[1024,512]{1,0:T(8,128)(2,1)S(1)} copy-done((bf16[1024,512]{1,0:T(8,128)(2,1)S(1)}, bf16[1024,512]{1,0:T(8,128)(2,1)}, u32[]{:S(2)}) %copy-start.2) | copy-done | bytes 1048600
  88.4 2.2 %downward.1 = f32[8,2,128,256]{3,2,1,0:T(8,128)} custom-call(f32[8,2,128,256]{3,2,1,0:T(8,128)S(1)} %get-tuple-element.35.near_ref, bf16[1024,512]{1,0:T(8,128)(2,1)S(1)} %copy-done.2, bf16[8,128,256]{2,1,0:T(8,128)(2,1)S(1)} %get-tuple-element.37.adjoint_ref, bf16[32,16,512]{2,1,0:T(8,128)(2,1)S(1)} %all-to-all-done.1.field_ref), custom_call_target="tpu_custom_call" | custom-call | flops 1000000 | bytes 1024 | tf_op jit(solution)/shard_map/downward/pallas_call | solution.py:491
  (38 shorter events, 0.8 us)
Async XLA Ops:
  0.0 16.7 %copy-start = (bf16[316,2,4,8]{0,3,2,1:T(8,128)(2,1)S(1)}, bf16[316,2,4,8]{0,3,2,1:T(8,128)(2,1)}, u32[]{:S(2)}) copy-start(bf16[316,2,4,8]{0,3,2,1:T(8,128)(2,1)} %param.19) | copy-start | bytes 121348
  1.7 8.4 %copy-start.8 = (bf16[8,2,128,256]{3,2,1,0:T(8,128)(2,1)S(1)}, bf16[8,2,128,256]{3,2,1,0:T(8,128)(2,1)}, u32[]{:S(2)}) copy-start(bf16[8,2,128,256]{3,2,1,0:T(8,128)(2,1)} %refs_3_.1) | copy-start | bytes 3145732
  7.0 9.0 %copy-start.9 = (s32[8,12]{1,0:T(8,128)S(1)}, s32[8,12]{1,0:T(8,128)}, u32[]{:S(2)}) copy-start(s32[8,12]{1,0:T(8,128)} %param.13) | copy-start | bytes 1156
  7.0 9.0 %copy-start.10 = (s32[8]{0:T(128)S(1)}, s32[8]{0:T(128)}, u32[]{:S(2)}) copy-start(s32[8]{0:T(128)} %param.14) | copy-start | bytes 100
  7.0 12.1 %collective-permute-start = (s32[256,2]{0,1:T(2,128)S(1)}, s32[256,2]{0,1:T(2,128)S(1)}, u32[]{:S(2)}, u32[]{:S(2)}) collective-permute-start(s32[256,2]{0,1:T(2,128)S(1)} %pad_add_fusion.2), channel_id=1, source_target_pairs={{0,16},{16,0},{1,17},{17,1},{2,18},{18,2},{3,19},{19,3},{4,20},{20... | collective-permute-start | bytes 6152 | tf_op jit(solution)/shard_map/ppermute | solution.py:535
  10.1 18.6 %collective-permute-start.2 = (bf16[4,2,128,256]{3,2,1,0:T(8,128)(2,1)S(1)}, bf16[4,2,128,256]{3,2,1,0:T(8,128)(2,1)S(1)}, u32[]{:S(2)}, u32[]{:S(2)}) collective-permute-start(bf16[4,2,128,256]{3,2,1,0:T(8,128)(2,1)S(1)} %get-tuple-element.26), channel_id=1, source_target_pairs={{1,0},{2,1},{3,2},{4,3},{5,4},{6,5},{7,6},{8,7},{9,8},{10,9},{11,1... | collective-permute-start | bytes 1572872 | tf_op jit(solution)/shard_map/ppermute | solution.py:513
  11.4 17.3 %collective-permute-start.1 = (bf16[4,2,128,256]{3,2,1,0:T(8,128)(2,1)S(1)}, bf16[4,2,128,256]{3,2,1,0:T(8,128)(2,1)S(1)}, u32[]{:S(2)}, u32[]{:S(2)}) collective-permute-start(bf16[4,2,128,256]{3,2,1,0:T(8,128)(2,1)S(1)} %get-tuple-element.27), channel_id=1, source_target_pairs={{0,1},{1,2},{2,3},{3,4},{4,5},{5,6},{6,7},{7,8},{8,9},{9,10},{10,1... | collective-permute-start | bytes 1572872 | tf_op jit(solution)/shard_map/ppermute | solution.py:513
  20.6 0.7 copy-start.3
  21.3 28.4 %all-to-all-start = ((bf16[32,16,512]{2,1,0:T(8,128)(2,1)}), bf16[32,16,512]{2,1,0:T(8,128)(2,1)S(1)}, u32[]{:S(2)}, u32[]{:S(2)}) async-start(bf16[32,16,512]{2,1,0:T(8,128)(2,1)} %upward.1), calls=%async_computation | async-start | bytes 1048576 | tf_op jit(solution)/shard_map/all_to_all | solution.py:524
  35.4 33.1 %collective-permute-start.3 = (bf16[4,2,128,256]{3,2,1,0:T(8,128)(2,1)S(1)}, bf16[4,2,128,256]{3,2,1,0:T(8,128)(2,1)S(1)}, u32[]{:S(2)}, u32[]{:S(2)}) collective-permute-start(bf16[4,2,128,256]{3,2,1,0:T(8,128)(2,1)S(1)} %get-tuple-element.26), channel_id=1, source_target_pairs={{0,1},{1,2},{2,3},{3,4},{4,5},{5,6},{6,7},{7,8},{8,9},{9,10},{10,1... | collective-permute-start | bytes 1572872 | tf_op jit(solution)/shard_map/ppermute | solution.py:513
  44.7 26.6 %collective-permute-start.4 = (bf16[4,2,128,256]{3,2,1,0:T(8,128)(2,1)S(1)}, bf16[4,2,128,256]{3,2,1,0:T(8,128)(2,1)S(1)}, u32[]{:S(2)}, u32[]{:S(2)}) collective-permute-start(bf16[4,2,128,256]{3,2,1,0:T(8,128)(2,1)S(1)} %get-tuple-element.27), channel_id=1, source_target_pairs={{1,0},{2,1},{3,2},{4,3},{5,4},{6,5},{7,6},{8,7},{9,8},{10,9},{11,1... | collective-permute-start | bytes 1572872 | tf_op jit(solution)/shard_map/ppermute | solution.py:513
  52.2 34.9 %all-to-all-start.1 = ((bf16[32,16,512]{2,1,0:T(8,128)(2,1)}), bf16[32,16,512]{2,1,0:T(8,128)(2,1)S(1)}, u32[]{:S(2)}, u32[]{:S(2)}) async-start(bf16[32,16,512]{2,1,0:T(8,128)(2,1)} %translate.1), calls=%async_computation.1 | async-start | bytes 1048576 | tf_op jit(solution)/shard_map/all_to_all | solution.py:524
  68.6 0.8 copy-start.4
  71.3 0.8 copy-start.6
  72.1 1.0 %copy-start.5 = (bf16[4,2,128,256]{3,2,1,0:T(8,128)(2,1)S(1)}, bf16[4,2,128,256]{3,2,1,0:T(8,128)(2,1)}, u32[]{:S(2)}) copy-start(bf16[4,2,128,256]{3,2,1,0:T(8,128)(2,1)} %copy-done.4) | copy-start | bytes 1572868
  73.2 1.0 %copy-start.7 = (bf16[4,2,128,256]{3,2,1,0:T(8,128)(2,1)S(1)}, bf16[4,2,128,256]{3,2,1,0:T(8,128)(2,1)}, u32[]{:S(2)}) copy-start(bf16[4,2,128,256]{3,2,1,0:T(8,128)(2,1)} %copy-done.6) | copy-start | bytes 1572868
  79.9 1.0 %copy-start.1 = (bf16[1024,512]{1,0:T(8,128)(2,1)}, bf16[1024,512]{1,0:T(8,128)(2,1)S(1)}, u32[]{:S(2)}) copy-start(bf16[1024,512]{1,0:T(8,128)(2,1)S(1)} %get-tuple-element.36.w_ref) | copy-start | bytes 3145732
  87.2 1.2 %copy-start.2 = (bf16[1024,512]{1,0:T(8,128)(2,1)S(1)}, bf16[1024,512]{1,0:T(8,128)(2,1)}, u32[]{:S(2)}) copy-start(bf16[1024,512]{1,0:T(8,128)(2,1)} %copy-done.1) | copy-start | bytes 3145732
where the time goes:
time: 91.6 us; the launch traced here: 90.6 us
  starting transfers between devices  34.5 us (38%)
  Pallas kernels  34.1 us (37%)
  waiting for transfers between devices  11.9 us (13%)
  local copies, waits for them, and re-layouts  8.16 us (9%)
  other arithmetic  1.54 us (2%)
    pallas_call x3, Pallas kernels, near_field(): pl.pallas_call(kernel, in_specs=[smem] * 2 + [hbm] + [pl.BlockSpec(memory...  21 us
    ppermute x4, starting transfers between devices, shift(): return lax.ppermute(block, axis, pairs)  16.4 us
    all_to_all x2, starting transfers between devices, parent_bands(): return lax.all_to_all(spread, axes, split_axis=0, concat_axis=0, tiled=True)  15.1 us
    all_to_all x2, waiting for transfers between devices, parent_bands(): return lax.all_to_all(spread, axes, split_axis=0, concat_axis=0, tiled=True)  9.94 us
    unnamed x22, local copies, waits for them, and re-layouts  6.55 us
    pallas_call x1, Pallas kernels, upward(): pl.pallas_call(up_kernel, in_specs=[hbm] * 3, out_specs=hbm, out_shape=pl...  5.3 us
    ppermute x1, starting transfers between devices, translation_lines(): other = lax.ppermute(lists, 'box', [(0, 1), (1, 0)])  3 us
    pallas_call x1, Pallas kernels, translate(): pl.pallas_call(translate_kernel, in_specs=[hbm] + [anywhere] * len(source...  2.5 us
  transfers between devices with their start and end apart: 7, of which 3 were waited for; matrix products, arithmetic and copies ran while one was open for 2% of the time, Pallas kernels for 29%

commit v1 on v0

--- a/solution.py
+++ b/solution.py
@@ -450,17 +450,37 @@
     )(radiation)
 
 
-def down_kernel(near_ref, w_ref, adjoint_ref, field_ref, out_hbm, field, held, sems):
+def down_kernel(w_hbm, adjoint_hbm, near_hbm, field_ref, out_hbm, *scratch):
+    w_ref, adjoint_ref, field, held, sems = scratch
     boxes, _, width = adjoint_ref.shape
     points = width // 2
     rhs = held.shape[3]
-    field_copy = pltpu.make_async_copy(field_ref, field, sems.at[boxes])
+    rows = w_ref.shape[0] // boxes
+
+    def by_box(source, target, turn):
+        return [
+            pltpu.make_async_copy(source(box), target(box), sems.at[turn * boxes + box])
+            for box in range(boxes)
+        ]
+
+    w_copies = by_box(
+        lambda box: w_hbm.at[pl.ds(box * rows, rows)],
+        lambda box: w_ref.at[pl.ds(box * rows, rows)],
+        0,
+    )
+    adjoint_copies = by_box(lambda box: adjoint_hbm.at[box], lambda box: adjoint_ref.at[box], 1)
+    near_copies = by_box(lambda box: near_hbm.at[box], lambda box: held.at[box], 2)
+    out_copies = by_box(lambda box: held.at[box], lambda box: out_hbm.at[box], 3)
+    field_copy = pltpu.make_async_copy(field_ref, field, sems.at[4 * boxes])
     field_copy.start()
-    out_copies = [
-        pltpu.make_async_copy(held.at[box], out_hbm.at[box], sems.at[box]) for box in range(boxes)
-    ]
+    for copy in w_copies + adjoint_copies + near_copies:
+        copy.start()
     field_copy.wait()
+    for copy in w_copies:
+        copy.wait()
     mixed = dot(w_ref[...], field[...].reshape(w_ref.shape[1], 2 * rhs))
+    for copy in adjoint_copies + near_copies:
+        copy.wait()
     for octant in range(boxes // 2):
         start = 2 * octant * points
         cos_part = mixed[start : start + points]
@@ -475,8 +495,8 @@
             real, imag = real.astype(BF16), imag.astype(BF16)
             right = jnp.concatenate([side_by_side(real, imag), side_by_side(imag, -real)], axis=0)
             far = dot(adjoint_ref[box], right)
-            held[box, 0] = near_ref[box, 0] + far[:, :rhs]
-            held[box, 1] = near_ref[box, 1] + far[:, rhs:]
+            held[box, 0] += far[:, :rhs]
+            held[box, 1] += far[:, rhs:]
             out_copies[box].start()
     for copy in out_copies:
         copy.wait()
@@ -484,27 +504,25 @@
 
 def downward(field, near, weights, radiation_adjoint):
     boxes = near.shape[0]
-    ready = [
-        pltpu.with_memory_space_constraint(array, pltpu.VMEM)
-        for array in (near, weights, radiation_adjoint)
-    ]
+    hbm = pl.BlockSpec(memory_space=pltpu.HBM)
     return pl.pallas_call(
         down_kernel,
-        in_specs=[pl.BlockSpec(memory_space=pltpu.VMEM)] * 3
-        + [pl.BlockSpec(memory_space=pl.ANY)],
-        out_specs=pl.BlockSpec(memory_space=pltpu.HBM),
+        in_specs=[hbm] * 3 + [pl.BlockSpec(memory_space=pl.ANY)],
+        out_specs=hbm,
         out_shape=jax.ShapeDtypeStruct(near.shape, F32),
         scratch_shapes=[
+            pltpu.VMEM(weights.shape, BF16),
+            pltpu.VMEM(radiation_adjoint.shape, BF16),
             pltpu.VMEM(field.shape, BF16),
             pltpu.VMEM(near.shape, F32),
-            pltpu.SemaphoreType.DMA((boxes + 1,)),
+            pltpu.SemaphoreType.DMA((4 * boxes + 1,)),
         ],
         compiler_params=pltpu.CompilerParams(vmem_limit_bytes=32 * MIB),
         cost_estimate=pl.CostEstimate(
             flops=10**6, bytes_accessed=2**10, transcendentals=0
         ),
         name="downward",
-    )(*ready, field)
+    )(*in_hbm(weights, radiation_adjoint, near), field)
 
 
 def shift(block, axis, step):
@@ -564,14 +582,12 @@
     nearer = (shift(back, every, 1), shift(front, every, -1))
     spread = upward(coeffs, radiation, up_weights, shares * per_group)
     radiation_adjoint = adjoint(radiation)
+    spread, radiation_adjoint = lax.optimization_barrier((spread, radiation_adjoint))
+    parents = parent_bands(spread, shares)
     lists = lists_of(partners, vector_ids, pair_count)
-    spread, lists = lax.optimization_barrier((spread, lists))
     lines = translation_lines(lists, translation, shares, per_group)
     listed, starts = near_slots(near_ids, near_count, lax.axis_index(every))
-    spread, lines, radiation_adjoint, listed, starts = lax.optimization_barrier(
-        (spread, lines, radiation_adjoint, listed, starts)
-    )
-    parents = parent_bands(spread, shares)
+    lines, listed, starts = lax.optimization_barrier((lines, listed, starts))
     near = near_field(listed, starts, near_blocks, nearer, 0)
     near, front, back = lax.optimization_barrier((near, front, back))
     farther = (shift(front, every, 1), shift(back, every, -1))
@@ -583,10 +599,8 @@
     incoming, near = lax.optimization_barrier((incoming, near))
     field = parent_bands(incoming, shares)
     near = near_field(listed, starts, near_blocks, (coeffs,), 1, near)
-    ready = near_field(
-        listed, starts, near_blocks, farther, 2, near, keep=(down_weights, radiation_adjoint)
-    )
-    return downward(field, *ready)
+    near = near_field(listed, starts, near_blocks, farther, 2, near)
+    return downward(field, near, down_weights, radiation_adjoint)
 
 
 def solution(mesh):

time: 91.6 us -> 105 us (1.15)
  waiting for transfers between devices: 11.9 us -> 25.2 us
  local copies, waits for them, and re-layouts: 8.16 us -> 2.3 us
  starting transfers between devices: 34.5 us -> 39 us
  Pallas kernels: 34.1 us -> 35.8 us
    ppermute x4, waiting for transfers between devices: 2.01 us -> 21.7 us  [shift(): return lax.ppermute(block, axis, pairs)]
    ppermute x4, starting transfers between devices: 16.4 us -> 25 us  [shift(): return lax.ppermute(block, axis, pairs)]
    all_to_all x2, waiting for transfers between devices: 9.94 us -> 3.46 us  [parent_bands(): return lax.all_to_all(spread, axes, split_axis=0, concat_axis=0, tiled=True)]
    unnamed x22 -> x10, local copies, waits for them, and re-layouts: 6.55 us -> 0.67 us
    all_to_all x2, starting transfers between devices: 15.1 us -> 11 us  [parent_bands(): return lax.all_to_all(spread, axes, split_axis=0, concat_axis=0, tiled=True)]
    pallas_call x1, Pallas kernels: 2.17 us -> 3.93 us  [downward(): pl.pallas_call(down_kernel, in_specs=[hbm] * 3 + [pl.BlockSpec(memory_spa...]
  transfers between devices with their start and end apart: 7 -> 7, of which waited for: 3 -> 3; matrix products, arithmetic and copies ran while one was open for 2% -> 1% of each run, Pallas kernels for 29% -> 31%
where the time goes in v1:
time: 105 us; the launch traced here: 104 us
  starting transfers between devices  39 us (37%)
  Pallas kernels  35.8 us (34%)
  waiting for transfers between devices  25.2 us (24%)
  local copies, waits for them, and re-layouts  2.3 us (2%)
  other arithmetic  1.55 us (1%)
    ppermute x4, starting transfers between devices, shift(): return lax.ppermute(block, axis, pairs)  25 us
    ppermute x4, waiting for transfers between devices, shift(): return lax.ppermute(block, axis, pairs)  21.7 us
    pallas_call x3, Pallas kernels, near_field(): pl.pallas_call(kernel, in_specs=[smem] * 2 + [hbm] + [pl.BlockSpec(memory...  21 us
    all_to_all x2, starting transfers between devices, parent_bands(): return lax.all_to_all(spread, axes, split_axis=0, concat_axis=0, tiled=True)  11 us
    pallas_call x1, Pallas kernels, upward(): pl.pallas_call(up_kernel, in_specs=[hbm] * 3, out_specs=hbm, out_shape=pl...  5.3 us
    pallas_call x1, Pallas kernels, downward(): pl.pallas_call(down_kernel, in_specs=[hbm] * 3 + [pl.BlockSpec(memory_spa...  3.93 us
    all_to_all x2, waiting for transfers between devices, parent_bands(): return lax.all_to_all(spread, axes, split_axis=0, concat_axis=0, tiled=True)  3.46 us
    ppermute x1, starting transfers between devices, translation_lines(): other = lax.ppermute(lists, 'box', [(0, 1), (1, 0)])  3 us
  transfers between devices with their start and end apart: 7, of which 3 were waited for; matrix products, arithmetic and copies ran while one was open for 1% of the time, Pallas kernels for 31%

profile of v1, /device:TPU:0, one launch (start us, length us, event | category | flops | bytes accessed | tf_op | source)
XLA Modules:
  0.0 104.1 jit_solution(1111056991700241428)
XLA Ops:
  0.0 0.8 stack.16
  0.8 0.8 fusion.1
  1.6 0.1 stack.15
  1.7 3.0 %collective-permute-start = (s32[256,2]{0,1:T(2,128)S(1)}, s32[256,2]{0,1:T(2,128)S(1)}, u32[]{:S(2)}, u32[]{:S(2)}) collective-permute-start(s32[256,2]{0,1:T(2,128)S(1)} %pad_add_fusion.1), channel_id=1, source_target_pairs={{0,16},{16,0},{1,17},{17,1},{2,18},{18,2},{3,19},{19,3},{4,20},{20... | collective-permute-start | bytes 6152 | tf_op jit(solution)/shard_map/ppermute | solution.py:553
  4.7 2.0 %adjoint.1.adjoint_hbm = bf16[8,128,256]{2,1,0:T(8,128)(2,1)} custom-call(bf16[8,2,128,128]{3,2,1,0:T(8,128)(2,1)} %rad_ref.1), custom_call_target="tpu_custom_call" | custom-call | flops 1000000 | bytes 1024 | tf_op jit(solution)/shard_map/adjoint/pallas_call | solution.py:440
  6.7 5.3 %upward.1 = bf16[32,16,512]{2,1,0:T(8,128)(2,1)} custom-call(bf16[8,2,128,256]{3,2,1,0:T(8,128)(2,1)} %refs_3_.1, bf16[8,2,128,128]{3,2,1,0:T(8,128)(2,1)} %rad_ref.1, bf16[1024,1024]{1,0:T(8,128)(2,1)} %constant.77.clone.w_hbm), custom_call_target="tpu_custom_call" | custom-call | flops 1000000 | bytes 1024 | tf_op jit(solution)/shard_map/upward/pallas_call | solution.py:127
  12.0 4.9 %all-to-all-start = ((bf16[32,16,512]{2,1,0:T(8,128)(2,1)}), bf16[32,16,512]{2,1,0:T(8,128)(2,1)S(1)}, u32[]{:S(2)}, u32[]{:S(2)}) async-start(bf16[32,16,512]{2,1,0:T(8,128)(2,1)} %upward.1), calls=%async_computation | async-start | bytes 1048576 | tf_op jit(solution)/shard_map/all_to_all | solution.py:542
  17.0 0.1 fusion.4
  17.1 1.3 %collective-permute-start.2 = (bf16[4,2,128,256]{3,2,1,0:T(8,128)(2,1)S(1)}, bf16[4,2,128,256]{3,2,1,0:T(8,128)(2,1)S(1)}, u32[]{:S(2)}, u32[]{:S(2)}) collective-permute-start(bf16[4,2,128,256]{3,2,1,0:T(8,128)(2,1)S(1)} %get-tuple-element.20), channel_id=1, source_target_pairs={{1,0},{2,1},{3,2},{4,3},{5,4},{6,5},{7,6},{8,7},{9,8},{10,9},{11,1... | collective-permute-start | bytes 1572872 | tf_op jit(solution)/shard_map/ppermute | solution.py:531
  18.4 4.6 %collective-permute-start.1 = (bf16[4,2,128,256]{3,2,1,0:T(8,128)(2,1)S(1)}, bf16[4,2,128,256]{3,2,1,0:T(8,128)(2,1)S(1)}, u32[]{:S(2)}, u32[]{:S(2)}) collective-permute-start(bf16[4,2,128,256]{3,2,1,0:T(8,128)(2,1)S(1)} %get-tuple-element.21), channel_id=1, source_target_pairs={{0,1},{1,2},{2,3},{3,4},{4,5},{5,6},{6,7},{7,8},{8,9},{9,10},{10,1... | collective-permute-start | bytes 1572872 | tf_op jit(solution)/shard_map/ppermute | solution.py:531
  23.1 0.1 reshape.292
  23.2 0.1 reshape.293
  23.4 0.1 convert_reduce_fusion
  23.5 0.2 select_reduce_fusion.refs_0_
  23.7 0.2 convert_reduce_fusion.1
  23.9 0.1 copy.21.table_ref
  24.1 0.1 copy.20
  24.2 0.1 copy.19
  24.4 1.1 %coupling.1.lines_hbm = f32[2,32,512]{2,1,0:T(8,128)S(1)} custom-call(s32[512,2]{1,0:T(8,128)S(1)} %broadcast_select_fusion.lists_ref, s32[1]{0:T(128)} %constant.65.clone.1.base_ref, bf16[316,32]{1,0:T(8,128)(2,1)S(1)} %copy.21.table_ref), custom_call_target="tpu_custom_call" | custom-call | flops 200000000 | bytes 2097152 | tf_op jit(solution)/shard_map/coupling/pallas_call | solution.py:175
  25.5 0.6 copy-done.1
  26.2 0.1 copy.24.refs_1_
  26.3 13.2 %collective-permute-done.2.refs_4_ = bf16[4,2,128,256]{3,2,1,0:T(8,128)(2,1)S(1)} collective-permute-done((bf16[4,2,128,256]{3,2,1,0:T(8,128)(2,1)S(1)}, bf16[4,2,128,256]{3,2,1,0:T(8,128)(2,1)S(1)}, u32[]{:S(2)}, u32[]{:S(2)}) %collective-permute-start.2) | collective-permute-done | bytes 524320 | tf_op jit(solution)/shard_map/ppermute | solution.py:531
  39.5 6.6 %near_nearer.1.refs_4_ = f32[8,2,128,256]{3,2,1,0:T(8,128)} custom-call(s32[3,96]{1,0:T(4,128)S(1)} %select_reduce_fusion.refs_0_, s32[3,9]{1,0:T(4,128)S(1)} %copy.24.refs_1_, bf16[96,2,128,128]{3,2,1,0:T(8,128)(2,1)} %bitcast.2, bf16[4,2,128,256]{3,2,1,0:T(8,128)(2,1)S(1)} %collective-permute-done.1.refs_3_, ...), custom_call_target="tpu_custom_call" | custom-call | flops 99999997952 | bytes 1024 | tf_op jit(solution)/shard_map/near_nearer/pallas_call | solution.py:404
  46.1 17.9 %collective-permute-start.3 = (bf16[4,2,128,256]{3,2,1,0:T(8,128)(2,1)S(1)}, bf16[4,2,128,256]{3,2,1,0:T(8,128)(2,1)S(1)}, u32[]{:S(2)}, u32[]{:S(2)}) collective-permute-start(bf16[4,2,128,256]{3,2,1,0:T(8,128)(2,1)S(1)} %get-tuple-element.20), channel_id=1, source_target_pairs={{0,1},{1,2},{2,3},{3,4},{4,5},{5,6},{6,7},{7,8},{8,9},{9,10},{10,1... | collective-permute-start | bytes 1572872 | tf_op jit(solution)/shard_map/ppermute | solution.py:531
  64.0 1.3 %collective-permute-start.4 = (bf16[4,2,128,256]{3,2,1,0:T(8,128)(2,1)S(1)}, bf16[4,2,128,256]{3,2,1,0:T(8,128)(2,1)S(1)}, u32[]{:S(2)}, u32[]{:S(2)}) collective-permute-start(bf16[4,2,128,256]{3,2,1,0:T(8,128)(2,1)S(1)} %get-tuple-element.21), channel_id=1, source_target_pairs={{1,0},{2,1},{3,2},{4,3},{5,4},{6,5},{7,6},{8,7},{9,8},{10,9},{11,1... | collective-permute-start | bytes 1572872 | tf_op jit(solution)/shard_map/ppermute | solution.py:531
  65.3 2.5 %translate.1 = bf16[32,16,512]{2,1,0:T(8,128)(2,1)} custom-call(f32[2,32,512]{2,1,0:T(8,128)} %copy-done.1, bf16[32,16,512]{2,1,0:T(8,128)(2,1)S(1)} %all-to-all-done.refs_0_), custom_call_target="tpu_custom_call" | custom-call | flops 1000000 | bytes 1024 | tf_op jit(solution)/shard_map/translate/pallas_call | solution.py:230
  67.8 6.1 %all-to-all-start.1 = ((bf16[32,16,512]{2,1,0:T(8,128)(2,1)}), bf16[32,16,512]{2,1,0:T(8,128)(2,1)S(1)}, u32[]{:S(2)}, u32[]{:S(2)}) async-start(bf16[32,16,512]{2,1,0:T(8,128)(2,1)} %translate.1), calls=%async_computation.1 | async-start | bytes 1048576 | tf_op jit(solution)/shard_map/all_to_all | solution.py:542
  73.9 7.5 %near_own.1.refs_5_ = f32[8,2,128,256]{3,2,1,0:T(8,128)} custom-call(s32[3,96]{1,0:T(4,128)S(1)} %select_reduce_fusion.refs_0_, s32[3,9]{1,0:T(4,128)S(1)} %copy.24.refs_1_, bf16[96,2,128,128]{3,2,1,0:T(8,128)(2,1)} %bitcast.3, bf16[8,2,128,256]{3,2,1,0:T(8,128)(2,1)} %refs_3_.1, f32[8,2,128,256]{3,2,1,0:T(8,128)} %near_nearer.1.refs_4_), custom_call_target="tpu_custom_call" | custom-call | flops 1000000 | bytes 1024 | tf_op jit(solution)/shard_map/near_own/pallas_call | solution.py:404
  81.4 8.5 %collective-permute-done.4.refs_4_ = bf16[4,2,128,256]{3,2,1,0:T(8,128)(2,1)S(1)} collective-permute-done((bf16[4,2,128,256]{3,2,1,0:T(8,128)(2,1)S(1)}, bf16[4,2,128,256]{3,2,1,0:T(8,128)(2,1)S(1)}, u32[]{:S(2)}, u32[]{:S(2)}) %collective-permute-start.4) | collective-permute-done | bytes 524320 | tf_op jit(solution)/shard_map/ppermute | solution.py:531
  89.9 6.8 %near_farther.1.near_hbm = f32[8,2,128,256]{3,2,1,0:T(8,128)} custom-call(s32[3,96]{1,0:T(4,128)S(1)} %select_reduce_fusion.refs_0_, s32[3,9]{1,0:T(4,128)S(1)} %copy.24.refs_1_, bf16[96,2,128,128]{3,2,1,0:T(8,128)(2,1)} %bitcast.4, bf16[4,2,128,256]{3,2,1,0:T(8,128)(2,1)S(1)} %collective-permute-done.3.refs_3_, ...), custom_call_target="tpu_custom_call" | custom-call | flops 99999997952 | bytes 1024 | tf_op jit(solution)/shard_map/near_farther/pallas_call | solution.py:404
  96.7 3.5 %all-to-all-done.1.field_ref = bf16[32,16,512]{2,1,0:T(8,128)(2,1)S(1)} async-done(((bf16[32,16,512]{2,1,0:T(8,128)(2,1)}), bf16[32,16,512]{2,1,0:T(8,128)(2,1)S(1)}, u32[]{:S(2)}, u32[]{:S(2)}) %all-to-all-start.1) | async-done | bytes 524320 | tf_op jit(solution)/shard_map/all_to_all | solution.py:542
  100.2 3.9 %downward.1 = f32[8,2,128,256]{3,2,1,0:T(8,128)} custom-call(bf16[1024,512]{1,0:T(8,128)(2,1)} %constant.78.clone.w_hbm, bf16[8,128,256]{2,1,0:T(8,128)(2,1)} %adjoint.1.adjoint_hbm, f32[8,2,128,256]{3,2,1,0:T(8,128)} %near_farther.1.near_hbm, bf16[32,16,512]{2,1,0:T(8,128)(2,1)S(1)} %all-to-all-done.1.field_ref), custom_call_target="tpu_custom_call" | custom-call | flops 1000000 | bytes 1024 | tf_op jit(solution)/shard_map/downward/pallas_call | solution.py:508
  (26 shorter events, 0.3 us)
Async XLA Ops:
  0.0 23.7 %copy-start = (bf16[316,2,4,8]{0,3,2,1:T(8,128)(2,1)S(1)}, bf16[316,2,4,8]{0,3,2,1:T(8,128)(2,1)}, u32[]{:S(2)}) copy-start(bf16[316,2,4,8]{0,3,2,1:T(8,128)(2,1)} %param.19) | copy-start | bytes 121348
  1.7 22.4 %collective-permute-start = (s32[256,2]{0,1:T(2,128)S(1)}, s32[256,2]{0,1:T(2,128)S(1)}, u32[]{:S(2)}, u32[]{:S(2)}) collective-permute-start(s32[256,2]{0,1:T(2,128)S(1)} %pad_add_fusion.1), channel_id=1, source_target_pairs={{0,16},{16,0},{1,17},{17,1},{2,18},{18,2},{3,19},{19,3},{4,20},{20... | collective-permute-start | bytes 6152 | tf_op jit(solution)/shard_map/ppermute | solution.py:553
  6.7 10.3 %copy-start.2 = (bf16[8,2,128,256]{3,2,1,0:T(8,128)(2,1)S(1)}, bf16[8,2,128,256]{3,2,1,0:T(8,128)(2,1)}, u32[]{:S(2)}) copy-start(bf16[8,2,128,256]{3,2,1,0:T(8,128)(2,1)} %refs_3_.1) | copy-start | bytes 3145732
  12.0 11.0 %copy-start.3 = (s32[8,12]{1,0:T(8,128)S(1)}, s32[8,12]{1,0:T(8,128)}, u32[]{:S(2)}) copy-start(s32[8,12]{1,0:T(8,128)} %param.13) | copy-start | bytes 1156
  12.0 11.0 %copy-start.4 = (s32[8]{0:T(128)S(1)}, s32[8]{0:T(128)}, u32[]{:S(2)}) copy-start(s32[8]{0:T(128)} %param.14) | copy-start | bytes 100
  12.0 53.3 %all-to-all-start = ((bf16[32,16,512]{2,1,0:T(8,128)(2,1)}), bf16[32,16,512]{2,1,0:T(8,128)(2,1)S(1)}, u32[]{:S(2)}, u32[]{:S(2)}) async-start(bf16[32,16,512]{2,1,0:T(8,128)(2,1)} %upward.1), calls=%async_computation | async-start | bytes 1048576 | tf_op jit(solution)/shard_map/all_to_all | solution.py:542
  17.1 22.4 %collective-permute-start.2 = (bf16[4,2,128,256]{3,2,1,0:T(8,128)(2,1)S(1)}, bf16[4,2,128,256]{3,2,1,0:T(8,128)(2,1)S(1)}, u32[]{:S(2)}, u32[]{:S(2)}) collective-permute-start(bf16[4,2,128,256]{3,2,1,0:T(8,128)(2,1)S(1)} %get-tuple-element.20), channel_id=1, source_target_pairs={{1,0},{2,1},{3,2},{4,3},{5,4},{6,5},{7,6},{8,7},{9,8},{10,9},{11,1... | collective-permute-start | bytes 1572872 | tf_op jit(solution)/shard_map/ppermute | solution.py:531
  18.4 21.1 %collective-permute-start.1 = (bf16[4,2,128,256]{3,2,1,0:T(8,128)(2,1)S(1)}, bf16[4,2,128,256]{3,2,1,0:T(8,128)(2,1)S(1)}, u32[]{:S(2)}, u32[]{:S(2)}) collective-permute-start(bf16[4,2,128,256]{3,2,1,0:T(8,128)(2,1)S(1)} %get-tuple-element.21), channel_id=1, source_target_pairs={{0,1},{1,2},{2,3},{3,4},{4,5},{5,6},{6,7},{7,8},{8,9},{9,10},{10,1... | collective-permute-start | bytes 1572872 | tf_op jit(solution)/shard_map/ppermute | solution.py:531
  25.5 0.6 copy-start.1
  46.1 35.3 %collective-permute-start.3 = (bf16[4,2,128,256]{3,2,1,0:T(8,128)(2,1)S(1)}, bf16[4,2,128,256]{3,2,1,0:T(8,128)(2,1)S(1)}, u32[]{:S(2)}, u32[]{:S(2)}) collective-permute-start(bf16[4,2,128,256]{3,2,1,0:T(8,128)(2,1)S(1)} %get-tuple-element.20), channel_id=1, source_target_pairs={{0,1},{1,2},{2,3},{3,4},{4,5},{5,6},{6,7},{7,8},{8,9},{9,10},{10,1... | collective-permute-start | bytes 1572872 | tf_op jit(solution)/shard_map/ppermute | solution.py:531
  64.0 25.9 %collective-permute-start.4 = (bf16[4,2,128,256]{3,2,1,0:T(8,128)(2,1)S(1)}, bf16[4,2,128,256]{3,2,1,0:T(8,128)(2,1)S(1)}, u32[]{:S(2)}, u32[]{:S(2)}) collective-permute-start(bf16[4,2,128,256]{3,2,1,0:T(8,128)(2,1)S(1)} %get-tuple-element.21), channel_id=1, source_target_pairs={{1,0},{2,1},{3,2},{4,3},{5,4},{6,5},{7,6},{8,7},{9,8},{10,9},{11,1... | collective-permute-start | bytes 1572872 | tf_op jit(solution)/shard_map/ppermute | solution.py:531
  67.8 32.3 %all-to-all-start.1 = ((bf16[32,16,512]{2,1,0:T(8,128)(2,1)}), bf16[32,16,512]{2,1,0:T(8,128)(2,1)S(1)}, u32[]{:S(2)}, u32[]{:S(2)}) async-start(bf16[32,16,512]{2,1,0:T(8,128)(2,1)} %translate.1), calls=%async_computation.1 | async-start | bytes 1048576 | tf_op jit(solution)/shard_map/all_to_all | solution.py:542
